TPU v7x, 256 devices: a whole 4x4x8 slice. The times are simulated.
256 devices in a mesh: seq: 8 (over y, core), ep: 32 (over x, z).
Axes of the slice: x: 4, y: 4, z: 8, core: 2. Of those that a mesh axis runs over, the one named last changes fastest.
Arguments:
- entering: bfloat16 [32, 32, 7168], P('ep', 'seq'), may hold values from -6 to 6
- moe_gain: float32 [7168], replicated, may hold values from 0.1 to 1.9
- expert_ids: int32 [32, 32, 8], P('ep'), may hold values from 0 to 31, all different within a row; in each aligned block of 4 rows (0 to 3, 4 to 7, ..., all dimensions but the last counted through in order) at most 2 rows name the same one
- gate_weights: float32 [32, 32, 8], P('ep'), may hold values from 0.05 to 0.5
- w_gate: bfloat16 [32, 7168, 2048], P('ep', None, 'seq'), may hold values from -0.0625 to 0.0625
- w_up: bfloat16 [32, 7168, 2048], P('ep', None, 'seq'), may hold values from -0.0625 to 0.0625
- w_down: bfloat16 [32, 2048, 7168], P('ep', 'seq'), may hold values from -0.125 to 0.125
- w_latent: bfloat16 [7168, 512], P('seq'), may hold values from -0.0625 to 0.0625
- w_rope: bfloat16 [64, 7168], P(None, 'seq'), may hold values from -0.0625 to 0.0625
- latent_gain: float32 [512], replicated, may hold values from 0.1 to 1.9
- prefix_len: int32 [32], P('ep'), may hold values from 128 to 1024, as said below
- cache_latent: bfloat16 [32, 1024, 512], P('ep', 'seq'), may hold values from -4 to 4
- cache_rope: bfloat16 [32, 64, 1024], P('ep', None, 'seq'), may hold values from -4 to 4
- query_latent: bfloat16 [32, 32, 65536], P('ep', 'seq'), may hold values from -7 to 7
- query_rope: bfloat16 [32, 32, 8192], P('ep', 'seq'), may hold values from -32 to 32
Outputs:
- layer_out: bfloat16 [32, 32, 7168], P('ep', None, 'seq')
- attention: bfloat16 [32, 32, 65536], P('ep', 'seq')
Inputs may be any that keep to these rules, and one draw needn't show every extreme that they name: `expert_ids`: in each aligned block of 4 rows (one document's new tokens on one index of seq) no expert is named by more than 2 tokens, and in some blocks one is named by exactly 2. Each token names 8 different experts. `prefix_len`: some document has all 1024 positions cached.
All inputs are finite; a program needn't handle non-finite values.
Results may differ from a plain program's by a relative error of at most 0.018.
Values may be sent and summed in bfloat16 or wider, within the bound.
A program may use at most 128 MiB of HBM per device.

v0:
```python
import jax
import jax.numpy as jnp
from jax import lax
from jax.sharding import PartitionSpec as P

softmax_scale = 192 ** (-0.5)
rope_base = 10000.0


def rms_rows(values, gain):
    mean_sq = jnp.mean(values * values, axis=-1, keepdims=True)
    return values * lax.rsqrt(mean_sq + 1e-06) * gain


def rotate_pairs(values, positions):
    half = values.shape[-1] // 2
    steps = jnp.arange(half, dtype=jnp.float32) * 2.0 / values.shape[-1]
    freqs = rope_base ** (-steps)
    angle = positions.astype(jnp.float32)[:, None] * freqs[None, :]
    first = values[:, :half]
    second = values[:, half:]
    cosine = jnp.cos(angle)
    sine = jnp.sin(angle)
    return jnp.concatenate(
        [first * cosine - second * sine, second * cosine + first * sine], axis=-1
    )


def score_block(query_lat, query_rot, key_lat, key_rot_cols):
    lat_part = jnp.dot(query_lat, key_lat.T, preferred_element_type=jnp.float32)
    rot_part = jnp.dot(query_rot, key_rot_cols, preferred_element_type=jnp.float32)
    return (lat_part + rot_part) * softmax_scale


def block_slots(routes, experts, capacity):
    same = (routes[:, :, None, None] == routes[None, None, :, :]).any(axis=3)
    order = jnp.arange(routes.shape[0], dtype=jnp.int32)
    earlier = order[None, :] < order[:, None]
    slots = jnp.sum((same & earlier[:, None, :]).astype(jnp.int32), axis=2)
    return routes * capacity + slots


def expert_terms(rows, gate_matrix, up_matrix, down_matrix):
    gate = jnp.dot(rows, gate_matrix, preferred_element_type=jnp.float32)
    upper = jnp.dot(rows, up_matrix, preferred_element_type=jnp.float32)
    hidden = (jax.nn.silu(gate) * upper).astype(jnp.bfloat16)
    return jnp.dot(hidden, down_matrix, preferred_element_type=jnp.float32)


def local(
    entering,
    moe_gain,
    expert_ids,
    gate_weights,
    w_gate,
    w_up,
    w_down,
    w_latent,
    w_rope,
    latent_gain,
    prefix_len,
    cache_latent,
    cache_rope,
    query_latent,
    query_rope,
):
    seq_count = lax.axis_size("seq")
    seq_place = lax.axis_index("seq")
    experts = lax.axis_size("ep")
    own_entering = entering[0]
    new_dev, width = own_entering.shape
    new = new_dev * seq_count
    capacity = 2
    prefix = prefix_len[0]
    heads = query_latent.shape[2] // cache_latent.shape[2]
    lat_width = cache_latent.shape[2]
    rot_width = cache_rope.shape[1]
    routes = lax.dynamic_slice_in_dim(expert_ids[0], seq_place * new_dev, new_dev, 0)
    gates = lax.dynamic_slice_in_dim(gate_weights[0], seq_place * new_dev, new_dev, 0)
    normed = rms_rows(own_entering.astype(jnp.float32), moe_gain).astype(jnp.bfloat16)
    targets = block_slots(routes, experts, capacity)
    total_slots = experts * capacity
    hits = targets[:, :, None] == jnp.arange(total_slots, dtype=jnp.int32)[None, None, :]
    placement = jnp.any(hits, axis=1).astype(jnp.bfloat16)
    gate_rows = jnp.sum(jnp.where(hits, gates[:, :, None], 0.0), axis=1)
    outgoing = jnp.dot(placement.T, normed, preferred_element_type=jnp.float32)
    outgoing = outgoing.astype(jnp.bfloat16).reshape(experts, capacity, width)
    arrived = lax.all_to_all(outgoing, "ep", split_axis=0, concat_axis=0, tiled=True)
    rows = lax.all_gather(arrived.reshape(total_slots, width), "seq", axis=0, tiled=True)
    older_lat = lax.all_gather(cache_latent[0], "seq", axis=0, tiled=True)
    older_rot = lax.all_gather(cache_rope[0], "seq", axis=1, tiled=True)
    query_lat = query_latent[0].reshape(new_dev * heads, lat_width)
    query_rot = query_rope[0].reshape(new_dev * heads, rot_width)
    older = score_block(query_lat, query_rot, older_lat, older_rot)
    cache_ok = (jnp.arange(older_lat.shape[0], dtype=jnp.int32) < prefix)[None, :]
    older = jnp.where(cache_ok, older, -jnp.inf)
    older_high = jnp.max(older, axis=1)
    older_weights = jnp.exp(older - older_high[:, None])
    older_total = jnp.sum(older_weights, axis=1)
    older_sum = jnp.dot(
        older_weights.astype(jnp.bfloat16), older_lat, preferred_element_type=jnp.float32
    )
    terms = expert_terms(rows, w_gate[0], w_up[0], w_down[0]).astype(jnp.bfloat16)
    summed = lax.psum_scatter(terms, "seq", scatter_dimension=0, tiled=True)
    summed = summed.reshape(experts, capacity, width)
    returned = lax.all_to_all(summed, "ep", split_axis=0, concat_axis=0, tiled=True)
    weighted = jnp.dot(
        gate_rows,
        returned.reshape(total_slots, width).astype(jnp.float32),
        precision=lax.Precision.HIGHEST,
    )
    layer_own = (own_entering.astype(jnp.float32) + weighted).astype(jnp.bfloat16)
    layer = lax.all_to_all(layer_own, "seq", split_axis=1, concat_axis=0, tiled=True)
    latent_part = jnp.dot(layer, w_latent, preferred_element_type=jnp.float32)
    rope_part = lax.dot_general(
        layer, w_rope, (((1,), (1,)), ((), ())), preferred_element_type=jnp.float32
    )
    raw = lax.psum(jnp.concatenate([latent_part, rope_part], axis=1), "seq")
    fresh_lat = rms_rows(raw[:, :lat_width], latent_gain).astype(jnp.bfloat16)
    positions = prefix + jnp.arange(new, dtype=jnp.int32)
    fresh_rot = rotate_pairs(raw[:, lat_width:], positions).astype(jnp.bfloat16)
    fresh = score_block(query_lat, query_rot, fresh_lat, fresh_rot.T)
    query_place = seq_place * new_dev + jnp.arange(new_dev * heads, dtype=jnp.int32) // heads
    fresh_ok = jnp.arange(new, dtype=jnp.int32)[None, :] <= query_place[:, None]
    fresh = jnp.where(fresh_ok, fresh, -jnp.inf)
    highest = jnp.maximum(older_high, jnp.max(fresh, axis=1))
    scale = jnp.exp(older_high - highest)
    fresh_weights = jnp.exp(fresh - highest[:, None])
    total = older_total * scale + jnp.sum(fresh_weights, axis=1)
    gathered = older_sum * scale[:, None] + jnp.dot(
        fresh_weights.astype(jnp.bfloat16), fresh_lat, preferred_element_type=jnp.float32
    )
    output = (gathered / total[:, None]).astype(jnp.bfloat16).reshape(new_dev, heads * lat_width)
    return (layer[None], output[None])


def solution(mesh):
    placed = (
        P("ep", "seq", None),
        P(),
        P("ep", None, None),
        P("ep", None, None),
        P("ep", None, "seq"),
        P("ep", None, "seq"),
        P("ep", "seq", None),
        P("seq", None),
        P(None, "seq"),
        P(),
        P("ep"),
        P("ep", "seq", None),
        P("ep", None, "seq"),
        P("ep", "seq", None),
        P("ep", "seq", None),
    )
    return jax.shard_map(
        local,
        mesh=mesh,
        in_specs=placed,
        out_specs=(P("ep", None, "seq"), P("ep", "seq", None)),
        check_vma=False,
    )
```

profile of v0, /device:TPU:1, one launch (start us, length us, event | category | flops | bytes accessed | tf_op | source)
XLA Modules:
  0.0 291.2 jit_solution(7209616721143365374)
XLA Ops:
  7.2 0.0 copy-start
  7.2 0.0 all-gather.5.cloned.1.call-start
  7.2 0.8 constant_dynamic-slice_fusion.1
  8.1 0.1 copy.23
  8.2 0.4 compare_reduce_fusion
  8.6 0.1 convert_reduce_fusion
  8.7 0.1 fusion.47
  8.8 1.0 fusion.28
  9.8 1.3 convolution_convert_fusion.1
  11.1 0.3 reshape.118
  11.4 33.6 %all_to_all.29 = bf16[32,2,7168]{2,1,0:T(2,128)(2,1)S(1)} all-to-all(bf16[32,2,7168]{2,1,0:T(2,128)(2,1)S(1)} %reshape.118), channel_id=1, replica_groups=mesh['seq'=8,'ep'=32] {'ep'}, dimensions={0} | all-to-all | bytes 1835008 | tf_op jit(solution)/shard_map/all_to_all | solution.py:88
  45.0 1.3 reshape.119
  46.3 0.0 all-gather.5.cloned.1.call-update
  46.3 0.0 reduce-scatter.2.cloned.1.call-start
  46.4 49.3 %all-gather.5.cloned.1.call-done = bf16[512,7168]{1,0:T(8,128)(2,1)} async-done(((bf16[64,7168]{1,0:T(8,128)(2,1)}), bf16[512,7168]{1,0:T(8,128)(2,1)}) %all-gather.5.cloned.1.call-update) | async-done | bytes 7340048 | tf_op jit(solution)/shard_map/all_gather | solution.py:89
  95.7 6.2 %fusion.4 = f32[512,256]{1,0:T(8,128)S(1)} fusion(bf16[512,7168]{1,0:T(8,128)(2,1)} %all-gather.5.cloned.1.call-done, bf16[1,7168,256]{2,1,0:T(8,128)(2,1)} %param.19), kind=kOutput, calls=%fused_computation.7 | convolution fusion | flops 1879048192 | bytes 11534336 | tf_op jit(solution)/shard_map/dot_general | solution.py:44
  101.9 16.0 %convolution_convert_fusion = bf16[512,7168]{1,0:T(8,128)(2,1)} fusion(bf16[1,256,7168]{2,1,0:T(8,128)(2,1)} %param.21, bf16[512,7168]{1,0:T(8,128)(2,1)} %all-gather.5.cloned.1.call-done, bf16[1,7168,256]{2,1,0:T(8,128)(2,1)} %param.20, f32[512,256]{1,0:T(8,128)S(1)} %fusion.4), kind=kOutput, calls=%fused_computation | convolution fusion | flops 3762552832 | bytes 22544384 | tf_op jit(solution)/shard_map/dot_general | solution.py:47
  117.9 0.0 reduce-scatter.2.cloned.1.call-update
  117.9 0.0 copy-start.7
  117.9 0.0 copy-start.5
  117.9 0.0 copy-start.2
  118.0 0.0 copy-start.6
  118.0 49.3 %reduce-scatter.2.cloned.1.call-done = bf16[64,7168]{1,0:T(8,128)(2,1)} async-done(((bf16[512,7168]{1,0:T(8,128)(2,1)}), bf16[64,7168]{1,0:T(8,128)(2,1)}) %reduce-scatter.2.cloned.1.call-update) | async-done | bytes 917520 | tf_op jit(solution)/shard_map/reduce_scatter | solution.py:104
  167.2 3.1 %reshape.120 = bf16[32,2,7168]{2,1,0:T(2,128)(2,1)} reshape(bf16[64,7168]{1,0:T(8,128)(2,1)} %reduce-scatter.2.cloned.1.call-done) | data formatting | bytes 1835008 | tf_op jit(solution)/shard_map/reshape | solution.py:105
  170.3 9.7 %all-to-all-start.1 = ((bf16[32,2,7168]{2,1,0:T(2,128)(2,1)}), bf16[32,2,7168]{2,1,0:T(2,128)(2,1)S(1)}, u32[]{:S(2)}, u32[]{:S(2)}) async-start(bf16[32,2,7168]{2,1,0:T(2,128)(2,1)} %reshape.120), calls=%async_computation.2 | async-start | bytes 1835008 | tf_op jit(solution)/shard_map/all_to_all | solution.py:106
  180.0 0.2 all-gather.7.cloned.1.call-start
  180.2 0.5 all-gather.7.cloned.1.call-update
  180.7 0.0 copy-done.7
  180.7 0.1 constant_dynamic-slice_fusion
  180.8 0.1 copy.24
  180.9 0.0 copy-done.5
  180.9 0.2 reshape_squeeze.7
  181.1 0.0 copy-start.1
  181.1 0.4 reshape_squeeze.6
  182.2 12.7 %all-gather.1 = bf16[1,64,1024]{2,1,0:T(8,128)(2,1)S(1)} all-gather(bf16[1,64,128]{2,1,0:T(8,128)(2,1)S(1)} %copy-done.6), channel_id=3, replica_groups=mesh['seq'=8,'ep'=32] {'seq'}, dimensions={2}, use_global_device_ids=true | all-gather | bytes 147456 | tf_op jit(solution)/shard_map/all_gather | solution.py:91
  194.8 0.6 negate_power_fusion
  195.4 0.5 add_convert_fusion
  196.0 0.1 select_reduce_fusion
  196.1 1.8 fusion.26
  197.8 4.2 %all-to-all-done.1 = bf16[32,2,7168]{2,1,0:T(2,128)(2,1)S(1)} async-done(((bf16[32,2,7168]{2,1,0:T(2,128)(2,1)}), bf16[32,2,7168]{2,1,0:T(2,128)(2,1)S(1)}, u32[]{:S(2)}, u32[]{:S(2)}) %all-to-all-start.1) | async-done | bytes 917536 | tf_op jit(solution)/shard_map/all_to_all | solution.py:106
  202.0 0.3 reshape.121
  202.3 0.0 copy-done.3
  202.4 1.1 fusion
  203.5 8.9 %all-to-all-start.2 = ((bf16[4,8,896]{2,0,1:T(4,128)(2,1)}), bf16[4,8,896]{2,0,1:T(4,128)(2,1)}, u32[]{:S(2)}, u32[]{:S(2)}) async-start(bf16[4,8,896]{2,0,1:T(4,128)(2,1)} %bitcast.7), calls=%async_computation.3 | async-start | bytes 114688 | tf_op jit(solution)/shard_map/all_to_all | solution.py:113
  212.4 0.0 all-gather.7.cloned.1.call-done
  212.4 2.8 fusion.58
  215.2 2.1 all-to-all-done.2
  217.3 1.5 all_to_all.25
  218.8 1.1 fusion.61
  219.8 0.0 copy-done
  219.9 1.1 fusion.60
  220.9 0.7 pad_maximum_fusion
  221.6 0.0 all-reduce.2.cloned.1.call-update
  221.6 0.5 fusion.6
  222.1 1.5 broadcast_in_dim.34
  223.5 53.4 %all-reduce.2.cloned.1.call-done = f32[32,576]{1,0:T(8,128)} async-done(((f32[32,576]{1,0:T(8,128)}), f32[32,576]{1,0:T(8,128)}) %all-reduce.2.cloned.1.call-update) | async-done | bytes 73744 | tf_op jit(solution)/shard_map/psum | solution.py:118
  276.9 1.0 multiply_reduce_fusion
  278.0 1.1 fusion.57
  279.0 1.0 fusion.44
  280.0 1.1 fusion.59
  281.2 2.0 convolution_multiply_fusion
  283.2 0.0 copy-done.4
  283.2 0.3 fusion.9
  283.5 1.2 broadcast_in_dim_reshape.3
  (17 shorter events, 0.1 us)
Async XLA Ops:
  7.2 212.7 %copy-start = (bf16[896,512]{1,0:T(8,128)(2,1)S(1)}, bf16[896,512]{1,0:T(8,128)(2,1)}, u32[]{:S(2)}) copy-start(bf16[896,512]{1,0:T(8,128)(2,1)} %param.22) | copy-start | bytes 2752516
  7.2 88.5 %all-gather.5.cloned.1.call-start = ((), (), s32[]{:S(2)}) async-start(), calls=%async_computation.4 | async-start | bytes 8257536 | tf_op jit(solution)/shard_map/all_gather | solution.py:89
  46.3 120.9 %reduce-scatter.2.cloned.1.call-start = ((), (), s32[]{:S(2)}) async-start(), calls=%async_computation.5 | async-start | bytes 8257536 | tf_op jit(solution)/shard_map/reduce_scatter | solution.py:104
  117.9 62.8 %copy-start.7 = (f32[1,32,8]{1,2,0:T(8,128)S(1)}, f32[1,32,8]{1,2,0:T(8,128)}, u32[]{:S(2)}) copy-start(f32[1,32,8]{1,2,0:T(8,128)} %param.18) | copy-start | bytes 3076
  117.9 63.0 %copy-start.5 = (bf16[1,4,8192]{2,1,0:T(4,128)(2,1)S(1)}, bf16[1,4,8192]{2,1,0:T(4,128)(2,1)}, u32[]{:S(2)}) copy-start(bf16[1,4,8192]{2,1,0:T(4,128)(2,1)} %param.29) | copy-start | bytes 196612
  117.9 63.1 %copy-start.2 = (bf16[1,4,65536]{2,1,0:T(4,128)(2,1)S(1)}, bf16[1,4,65536]{2,1,0:T(4,128)(2,1)}, u32[]{:S(2)}) copy-start(bf16[1,4,65536]{2,1,0:T(4,128)(2,1)} %param.28) | copy-start | bytes 1572868
  118.0 64.2 %copy-start.6 = (bf16[1,64,128]{2,1,0:T(8,128)(2,1)S(1)}, bf16[1,64,128]{2,1,0:T(8,128)(2,1)}, u32[]{:S(2)}) copy-start(bf16[1,64,128]{2,1,0:T(8,128)(2,1)} %param.27) | copy-start | bytes 49156
  170.3 32.1 %copy-start.3 = (bf16[1,4,7168]{2,1,0:T(4,128)(2,1)S(1)}, bf16[1,4,7168]{2,1,0:T(4,128)(2,1)}, u32[]{:S(2)}) copy-start(bf16[1,4,7168]{2,1,0:T(4,128)(2,1)} %param.15) | copy-start | bytes 172036
  170.3 31.7 %all-to-all-start.1 = ((bf16[32,2,7168]{2,1,0:T(2,128)(2,1)}), bf16[32,2,7168]{2,1,0:T(2,128)(2,1)S(1)}, u32[]{:S(2)}, u32[]{:S(2)}) async-start(bf16[32,2,7168]{2,1,0:T(2,128)(2,1)} %reshape.120), calls=%async_computation.2 | async-start | bytes 1835008 | tf_op jit(solution)/shard_map/all_to_all | solution.py:106
  180.0 32.4 %all-gather.7.cloned.1.call-start = ((), (), s32[]{:S(2)}) async-start(), calls=%async_computation.7 | async-start | bytes 1179648 | tf_op jit(solution)/shard_map/all_gather | solution.py:90
  181.1 16.8 %copy-start.1 = (bf16[512,64]{1,0:T(8,128)(2,1)}, bf16[512,64]{1,0:T(8,128)(2,1)S(1)}, u32[]{:S(2)}) copy-start(bf16[512,64]{1,0:T(8,128)(2,1)S(1)} %reshape_squeeze.7) | copy-start | bytes 196612
  203.5 13.8 %all-to-all-start.2 = ((bf16[4,8,896]{2,0,1:T(4,128)(2,1)}), bf16[4,8,896]{2,0,1:T(4,128)(2,1)}, u32[]{:S(2)}, u32[]{:S(2)}) async-start(bf16[4,8,896]{2,0,1:T(4,128)(2,1)} %bitcast.7), calls=%async_computation.3 | async-start | bytes 114688 | tf_op jit(solution)/shard_map/all_to_all | solution.py:113
  212.4 65.6 %copy-start.8 = (f32[512]{0:T(512)S(1)}, f32[512]{0:T(512)}, u32[]{:S(2)}) copy-start(f32[512]{0:T(512)} %param.24) | copy-start | bytes 6148
  212.4 64.5 %all-reduce.2.cloned.1.call-start = ((), (), s32[]{:S(2)}) async-start(), calls=%async_computation.6 | async-start | bytes 163840 | tf_op jit(solution)/shard_map/psum | solution.py:118
  276.9 6.3 %copy-start.4 = (f32[32,576]{1,0:T(8,128)S(1)}, f32[32,576]{1,0:T(8,128)}, u32[]{:S(2)}) copy-start(f32[32,576]{1,0:T(8,128)} %all-reduce.2.cloned.1.call-done) | copy-start | bytes 221188
Sparse Core Ops, SparseCore 0:
  46.5 49.1 all-gather.4
  118.0 49.1 reduce-scatter.1
  182.7 26.2 all-gather.6
  221.7 55.1 all-reduce.1
where the time goes:
time: 292 us; the launch traced here: 291 us
  waiting for transfers between devices  159 us (54%)
  blocking collectives  46.3 us (16%)
  matrix products  35.8 us (12%)
  starting transfers between devices  18.9 us (6%)
  between operations  14.6 us (5%)
  local copies, waits for them, and re-layouts  10.8 us (4%)
  other arithmetic  6.02 us (2%)
    psum x1, waiting for transfers between devices, local(): raw = lax.psum(jnp.concatenate([latent_part, rope_part], axis=1), 'seq')  53.4 us
    all_gather x1, waiting for transfers between devices, local(): lax.all_gather(arrived.reshape(total_slots, width), 'seq', axis=0, tiled=...  49.3 us
    reduce_scatter x1, waiting for transfers between devices, local(): summed = lax.psum_scatter(terms, 'seq', scatter_dimension=0, tiled=True)  49.3 us
    all_to_all x1, blocking collectives, local(): lax.all_to_all(outgoing, 'ep', split_axis=0, concat_axis=0, tiled=True)  33.6 us
    dot_general x1, matrix products, expert_terms(): return jnp.dot(hidden, down_matrix, preferred_element_type=jnp.float32)  16 us
    all_gather x1, blocking collectives, local(): older_rot = lax.all_gather(cache_rope[0], 'seq', axis=1, tiled=True)  12.7 us
    all_to_all x1, starting transfers between devices, local(): lax.all_to_all(summed, 'ep', split_axis=0, concat_axis=0, tiled=True)  9.67 us
    all_to_all x1, starting transfers between devices, local(): lax.all_to_all(layer_own, 'seq', split_axis=1, concat_axis=0, tiled=True)  8.91 us
  transfers between devices with their start and end apart: 6, of which 5 were waited for; matrix products, arithmetic and copies ran while one was open for 3% of the time, Pallas kernels for 0%

commit v1 on v0

--- a/solution.py
+++ b/solution.py
@@ -110,7 +110,10 @@
         precision=lax.Precision.HIGHEST,
     )
     layer_own = (own_entering.astype(jnp.float32) + weighted).astype(jnp.bfloat16)
-    layer = lax.all_to_all(layer_own, "seq", split_axis=1, concat_axis=0, tiled=True)
+    layer = jnp.concatenate(
+        lax.all_to_all(jnp.stack(jnp.split(layer_own, lax.axis_size("seq"), axis=1)), "seq", 0, 0),
+        axis=0,
+    )
     latent_part = jnp.dot(layer, w_latent, preferred_element_type=jnp.float32)
     rope_part = lax.dot_general(
         layer, w_rope, (((1,), (1,)), ((), ())), preferred_element_type=jnp.float32

time: 292 us -> 296 us (1.014)
  local copies, waits for them, and re-layouts: 10.8 us -> 15.6 us
    unnamed x18 -> x25, local copies, waits for them, and re-layouts: 0.06 us -> 4.25 us
  transfers between devices with their start and end apart: 6 -> 6, of which waited for: 5 -> 5; matrix products, arithmetic and copies ran while one was open for 3% -> 5% of each run, Pallas kernels for 0% -> 0%
where the time goes in v1:
time: 296 us; the launch traced here: 295 us
  waiting for transfers between devices  159 us (54%)
  blocking collectives  46.3 us (16%)
  matrix products  35.1 us (12%)
  starting transfers between devices  18.9 us (6%)
  local copies, waits for them, and re-layouts  15.6 us (5%)
  between operations  14.7 us (5%)
  other arithmetic  6.02 us (2%)
    psum x1, waiting for transfers between devices, local(): raw = lax.psum(jnp.concatenate([latent_part, rope_part], axis=1), 'seq')  53.3 us
    all_gather x1, waiting for transfers between devices, local(): lax.all_gather(arrived.reshape(total_slots, width), 'seq', axis=0, tiled=...  49.3 us
    reduce_scatter x1, waiting for transfers between devices, local(): summed = lax.psum_scatter(terms, 'seq', scatter_dimension=0, tiled=True)  49.3 us
    all_to_all x1, blocking collectives, local(): lax.all_to_all(outgoing, 'ep', split_axis=0, concat_axis=0, tiled=True)  33.6 us
    dot_general x1, matrix products, expert_terms(): return jnp.dot(hidden, down_matrix, preferred_element_type=jnp.float32)  16 us
    all_gather x1, blocking collectives, local(): older_rot = lax.all_gather(cache_rope[0], 'seq', axis=1, tiled=True)  12.7 us
    all_to_all x1, starting transfers between devices, local(): lax.all_to_all(summed, 'ep', split_axis=0, concat_axis=0, tiled=True)  9.67 us
    all_to_all x1, starting transfers between devices, local(): lax.all_to_all(jnp.stack(jnp.split(layer_own, lax.axis_size('seq'), axis=...  8.91 us
  transfers between devices with their start and end apart: 6, of which 5 were waited for; matrix products, arithmetic and copies ran while one was open for 5% of the time, Pallas kernels for 0%

profile of v1, /device:TPU:1, one launch (start us, length us, event | category | flops | bytes accessed | tf_op | source)
XLA Modules:
  0.0 295.4 jit_solution(15736161494422817048)
XLA Ops:
  7.2 0.0 copy-start
  7.2 0.0 all-gather.5.cloned.1.call-start
  7.2 0.8 constant_dynamic-slice_fusion.1
  8.1 0.1 copy.21
  8.2 0.4 compare_reduce_fusion
  8.6 0.1 convert_reduce_fusion
  8.7 0.1 fusion.47
  8.8 1.0 fusion.28
  9.8 1.3 convolution_convert_fusion.1
  11.1 0.3 reshape.117
  11.4 33.6 %all_to_all.15 = bf16[32,2,7168]{2,1,0:T(2,128)(2,1)S(1)} all-to-all(bf16[32,2,7168]{2,1,0:T(2,128)(2,1)S(1)} %reshape.117), channel_id=1, replica_groups=mesh['seq'=8,'ep'=32] {'ep'}, dimensions={0} | all-to-all | bytes 1835008 | tf_op jit(solution)/shard_map/all_to_all | solution.py:88
  45.0 1.3 reshape.118
  46.3 0.0 all-gather.5.cloned.1.call-update
  46.3 0.0 reduce-scatter.2.cloned.1.call-start
  46.4 49.3 %all-gather.5.cloned.1.call-done = bf16[512,7168]{1,0:T(8,128)(2,1)} async-done(((bf16[64,7168]{1,0:T(8,128)(2,1)}), bf16[512,7168]{1,0:T(8,128)(2,1)}) %all-gather.5.cloned.1.call-update) | async-done | bytes 7340048 | tf_op jit(solution)/shard_map/all_gather | solution.py:89
  95.7 6.2 %fusion.4 = f32[512,256]{1,0:T(8,128)S(1)} fusion(bf16[512,7168]{1,0:T(8,128)(2,1)} %all-gather.5.cloned.1.call-done, bf16[1,7168,256]{2,1,0:T(8,128)(2,1)} %param.19), kind=kOutput, calls=%fused_computation.7 | convolution fusion | flops 1879048192 | bytes 11534336 | tf_op jit(solution)/shard_map/dot_general | solution.py:44
  101.9 16.0 %convolution_convert_fusion = bf16[512,7168]{1,0:T(8,128)(2,1)} fusion(bf16[1,256,7168]{2,1,0:T(8,128)(2,1)} %param.21, bf16[512,7168]{1,0:T(8,128)(2,1)} %all-gather.5.cloned.1.call-done, bf16[1,7168,256]{2,1,0:T(8,128)(2,1)} %param.20, f32[512,256]{1,0:T(8,128)S(1)} %fusion.4), kind=kOutput, calls=%fused_computation | convolution fusion | flops 3762552832 | bytes 22544384 | tf_op jit(solution)/shard_map/dot_general | solution.py:47
  117.9 0.0 reduce-scatter.2.cloned.1.call-update
  117.9 0.0 copy-start.5
  118.0 49.3 %reduce-scatter.2.cloned.1.call-done = bf16[64,7168]{1,0:T(8,128)(2,1)} async-done(((bf16[512,7168]{1,0:T(8,128)(2,1)}), bf16[64,7168]{1,0:T(8,128)(2,1)}) %reduce-scatter.2.cloned.1.call-update) | async-done | bytes 917520 | tf_op jit(solution)/shard_map/reduce_scatter | solution.py:104
  167.2 3.1 %reshape.119 = bf16[32,2,7168]{2,1,0:T(2,128)(2,1)} reshape(bf16[64,7168]{1,0:T(8,128)(2,1)} %reduce-scatter.2.cloned.1.call-done) | data formatting | bytes 1835008 | tf_op jit(solution)/shard_map/reshape | solution.py:105
  170.3 9.7 %all-to-all-start.1 = ((bf16[32,2,7168]{2,1,0:T(2,128)(2,1)}), bf16[32,2,7168]{2,1,0:T(2,128)(2,1)S(1)}, u32[]{:S(2)}, u32[]{:S(2)}) async-start(bf16[32,2,7168]{2,1,0:T(2,128)(2,1)} %reshape.119), calls=%async_computation.2 | async-start | bytes 1835008 | tf_op jit(solution)/shard_map/all_to_all | solution.py:106
  180.0 0.2 all-gather.7.cloned.1.call-start
  180.2 0.5 all-gather.7.cloned.1.call-update
  180.7 0.1 constant_dynamic-slice_fusion
  180.8 0.1 copy.22
  180.9 0.2 reshape_squeeze.7
  181.1 0.4 reshape_squeeze.6
  182.2 12.7 %all-gather.1 = bf16[1,64,1024]{2,1,0:T(8,128)(2,1)S(1)} all-gather(bf16[1,64,128]{2,1,0:T(8,128)(2,1)S(1)} %copy-done.6), channel_id=3, replica_groups=mesh['seq'=8,'ep'=32] {'seq'}, dimensions={2}, use_global_device_ids=true | all-gather | bytes 147456 | tf_op jit(solution)/shard_map/all_gather | solution.py:91
  194.8 0.6 negate_power_fusion
  195.4 0.5 add_convert_fusion
  196.0 0.1 select_reduce_fusion
  196.1 1.8 fusion.26
  197.8 4.2 %all-to-all-done.1 = bf16[32,2,7168]{2,1,0:T(2,128)(2,1)S(1)} async-done(((bf16[32,2,7168]{2,1,0:T(2,128)(2,1)}), bf16[32,2,7168]{2,1,0:T(2,128)(2,1)S(1)}, u32[]{:S(2)}, u32[]{:S(2)}) %all-to-all-start.1) | async-done | bytes 917536 | tf_op jit(solution)/shard_map/all_to_all | solution.py:106
  202.0 0.3 reshape.120
  202.4 0.5 fusion
  202.8 0.6 constant_dynamic-update-slice_fusion.7
  203.4 0.6 constant_dynamic-update-slice_fusion.6
  204.0 0.6 constant_dynamic-update-slice_fusion.5
  204.6 0.6 constant_dynamic-update-slice_fusion.4
  205.2 0.6 constant_dynamic-update-slice_fusion.3
  205.8 0.6 constant_dynamic-update-slice_fusion.2
  206.4 0.6 constant_dynamic-update-slice_fusion.1
  207.0 0.6 constant_dynamic-update-slice_fusion
  207.6 8.9 %all-to-all-start.2 = ((bf16[8,4,896]{2,1,0:T(4,128)(2,1)}), bf16[8,4,896]{2,1,0:T(4,128)(2,1)}, u32[]{:S(2)}, u32[]{:S(2)}) async-start(bf16[8,4,896]{2,1,0:T(4,128)(2,1)} %constant_dynamic-update-slice_fusion), calls=%async_computation.3 | async-start | bytes 114688 | tf_op jit(solution)/shard_map/all_to_all | solution.py:114
  216.5 0.0 all-gather.7.cloned.1.call-done
  216.6 2.8 fusion.58
  219.3 2.1 all-to-all-done.2
  221.5 1.5 reshape.121
  222.9 1.1 fusion.61
  224.0 0.0 copy-done
  224.0 1.1 fusion.60
  225.1 0.7 pad_maximum_fusion
  225.7 0.0 all-reduce.2.cloned.1.call-update
  225.8 0.5 fusion.6
  226.2 1.5 broadcast_in_dim_reshape.6
  227.7 53.3 %all-reduce.2.cloned.1.call-done = f32[32,576]{1,0:T(8,128)} async-done(((f32[32,576]{1,0:T(8,128)}), f32[32,576]{1,0:T(8,128)}) %all-reduce.2.cloned.1.call-update) | async-done | bytes 73744 | tf_op jit(solution)/shard_map/psum | solution.py:121
  281.0 1.0 multiply_reduce_fusion
  282.1 1.1 fusion.57
  283.1 1.0 fusion.44
  284.1 1.1 fusion.59
  285.3 2.0 convolution_multiply_fusion
  287.3 0.3 fusion.9
  287.6 1.2 broadcast_in_dim_reshape.7
  (25 shorter events, 0.1 us)
Async XLA Ops:
  7.2 216.9 %copy-start = (bf16[896,512]{1,0:T(8,128)(2,1)S(1)}, bf16[896,512]{1,0:T(8,128)(2,1)}, u32[]{:S(2)}) copy-start(bf16[896,512]{1,0:T(8,128)(2,1)} %param.22) | copy-start | bytes 2752516
  7.2 88.5 %all-gather.5.cloned.1.call-start = ((), (), s32[]{:S(2)}) async-start(), calls=%async_computation.4 | async-start | bytes 8257536 | tf_op jit(solution)/shard_map/all_gather | solution.py:89
  46.3 120.9 %reduce-scatter.2.cloned.1.call-start = ((), (), s32[]{:S(2)}) async-start(), calls=%async_computation.5 | async-start | bytes 8257536 | tf_op jit(solution)/shard_map/reduce_scatter | solution.py:104
  117.9 62.8 %copy-start.7 = (f32[1,32,8]{1,2,0:T(8,128)S(1)}, f32[1,32,8]{1,2,0:T(8,128)}, u32[]{:S(2)}) copy-start(f32[1,32,8]{1,2,0:T(8,128)} %param.18) | copy-start | bytes 3076
  117.9 63.0 %copy-start.5 = (bf16[1,4,8192]{2,1,0:T(4,128)(2,1)S(1)}, bf16[1,4,8192]{2,1,0:T(4,128)(2,1)}, u32[]{:S(2)}) copy-start(bf16[1,4,8192]{2,1,0:T(4,128)(2,1)} %param.29) | copy-start | bytes 196612
  117.9 63.1 %copy-start.2 = (bf16[1,4,65536]{2,1,0:T(4,128)(2,1)S(1)}, bf16[1,4,65536]{2,1,0:T(4,128)(2,1)}, u32[]{:S(2)}) copy-start(bf16[1,4,65536]{2,1,0:T(4,128)(2,1)} %param.28) | copy-start | bytes 1572868
  118.0 64.2 %copy-start.6 = (bf16[1,64,128]{2,1,0:T(8,128)(2,1)S(1)}, bf16[1,64,128]{2,1,0:T(8,128)(2,1)}, u32[]{:S(2)}) copy-start(bf16[1,64,128]{2,1,0:T(8,128)(2,1)} %param.27) | copy-start | bytes 49156
  170.3 32.1 %copy-start.3 = (bf16[1,4,7168]{2,1,0:T(4,128)(2,1)S(1)}, bf16[1,4,7168]{2,1,0:T(4,128)(2,1)}, u32[]{:S(2)}) copy-start(bf16[1,4,7168]{2,1,0:T(4,128)(2,1)} %param.15) | copy-start | bytes 172036
  170.3 31.7 %all-to-all-start.1 = ((bf16[32,2,7168]{2,1,0:T(2,128)(2,1)}), bf16[32,2,7168]{2,1,0:T(2,128)(2,1)S(1)}, u32[]{:S(2)}, u32[]{:S(2)}) async-start(bf16[32,2,7168]{2,1,0:T(2,128)(2,1)} %reshape.119), calls=%async_computation.2 | async-start | bytes 1835008 | tf_op jit(solution)/shard_map/all_to_all | solution.py:106
  180.0 36.6 %all-gather.7.cloned.1.call-start = ((), (), s32[]{:S(2)}) async-start(), calls=%async_computation.7 | async-start | bytes 1179648 | tf_op jit(solution)/shard_map/all_gather | solution.py:90
  181.1 16.8 %copy-start.1 = (bf16[512,64]{1,0:T(8,128)(2,1)}, bf16[512,64]{1,0:T(8,128)(2,1)S(1)}, u32[]{:S(2)}) copy-start(bf16[512,64]{1,0:T(8,128)(2,1)S(1)} %reshape_squeeze.7) | copy-start | bytes 196612
  207.6 13.8 %all-to-all-start.2 = ((bf16[8,4,896]{2,1,0:T(4,128)(2,1)}), bf16[8,4,896]{2,1,0:T(4,128)(2,1)}, u32[]{:S(2)}, u32[]{:S(2)}) async-start(bf16[8,4,896]{2,1,0:T(4,128)(2,1)} %constant_dynamic-update-slice_fusion), calls=%async_computation.3 | async-start | bytes 114688 | tf_op jit(solution)/shard_map/all_to_all | solution.py:114
  216.5 65.5 %copy-start.8 = (f32[512]{0:T(512)S(1)}, f32[512]{0:T(512)}, u32[]{:S(2)}) copy-start(f32[512]{0:T(512)} %param.24) | copy-start | bytes 6148
  216.5 64.5 %all-reduce.2.cloned.1.call-start = ((), (), s32[]{:S(2)}) async-start(), calls=%async_computation.6 | async-start | bytes 163840 | tf_op jit(solution)/shard_map/psum | solution.py:121
  281.0 6.3 %copy-start.4 = (f32[32,576]{1,0:T(8,128)S(1)}, f32[32,576]{1,0:T(8,128)}, u32[]{:S(2)}) copy-start(f32[32,576]{1,0:T(8,128)} %all-reduce.2.cloned.1.call-done) | copy-start | bytes 221188
Sparse Core Ops, SparseCore 0:
  46.5 49.1 all-gather.4
  118.0 49.1 reduce-scatter.1
  182.7 26.2 all-gather.6
  225.9 55.0 all-reduce.1
